TPU v7x, 512 devices: a whole 4x8x8 slice. The times are simulated.
512 devices in a mesh: ctx: 64 (over y_lo, z, core), tp: 4 (over x), seq: 2 (over y_hi).
Axes of the slice: x: 4, y: 8 (y_hi: 2, y_lo: 4; y = y_hi * 4 + y_lo), z: 8, core: 2. Of those that a mesh axis runs over, the one named last changes fastest.
Arguments:
- queries: bfloat16 [2, 16384, 4096], P('seq', 'ctx', 'tp'), may hold values from -24 to 24
- attention_keys: bfloat16 [2, 16384, 512], P('seq', 'ctx', 'tp'), may hold values from -12 to 12
- attention_values: bfloat16 [2, 16384, 512], P('seq', 'ctx', 'tp'), may hold values from -6 to 6
- cotangent: bfloat16 [2, 16384, 4096], P('seq', 'ctx', 'tp'), may hold values from -6 to 6
- low_rank: bfloat16 [2, 16384, 128], P('seq', 'ctx'), may hold values from -22 to 22
- seq_lengths: int32 [2], replicated, may hold values from 8192 to 16384, as said below
- window_stops: int32 [2], replicated, may hold values from 128 to 768, as said below
- query_ids: int32 [512], replicated, may hold values from 0 to 511, each once
- query_up_gradients: float32 [512, 64, 4096], P('seq', 'ctx', 'tp'), may hold values from -6 to 6
- value_up_gradients: float32 [512, 64, 512], P('seq', 'ctx', 'tp'), may hold values from -6 to 6
Outputs:
- ranked: float32 [512, 2], replicated
Inputs may be any that keep to these rules, and one draw needn't show every extreme that they name: `seq_lengths`: some sequence has exactly 16384, and some other one fewer. `window_stops`: some sequence has exactly 768.
All inputs are finite; a program needn't handle non-finite values.
Results may differ from a plain program's by a relative error of at most 0.0056.
Values may be sent and summed in bfloat16 or wider, within the bound.
No kernel may reach another device: no remote copies, remote signals or barrier semaphores. Data moves between devices by JAX's collectives and lax.ppermute only.
A program may use at most 64 MiB of HBM per device.

v0:
```python
import functools

import jax
import jax.numpy as jnp
from jax import lax
from jax.experimental import pallas as pl
from jax.experimental.pallas import tpu as pltpu
from jax.sharding import Mesh
from jax.sharding import PartitionSpec as P

HEAD_SIZE = 128
WINDOW_BLOCKS = 3
TOKENS = 256
RANK = 64
HEADS = 8
KEYS = (WINDOW_BLOCKS + 1) * TOKENS
FEATURES = HEADS * HEAD_SIZE + HEAD_SIZE
HALF = 640
PACK = 2 * TOKENS + 128
CHUNK = 64
CHUNKS = [slice(i * CHUNK, (i + 1) * CHUNK) for i in range(KEYS // CHUNK)]
EARLY = 2
SHARE = 256
LINE = 2 * SHARE + 128
NEG_FILL = -1e30
SCALE = HEAD_SIZE ** (-0.5)
LOG2E = 1.4426950408889634

CTX = ("y", "z", "core")
VMEM = pl.BlockSpec(memory_space=pltpu.VMEM)
SMEM = pl.BlockSpec(memory_space=pltpu.SMEM)
NT = (((1,), (1,)), ((), ()))


def lanes(head):
    return slice(head * HEAD_SIZE, (head + 1) * HEAD_SIZE)


def folded(x):
    return x.reshape(x.shape[0] // 8, 8, TOKENS)


def visible_bias(place, stop):
    row = lax.broadcasted_iota(jnp.int32, (TOKENS, TOKENS), 0)
    col = lax.broadcasted_iota(jnp.int32, (TOKENS, TOKENS), 1)
    block, length, reach = place[0:1, :], place[1:2, :], place[2:3, :]
    gap = col - row + stop * TOKENS
    key_pos = (block - stop) * TOKENS + row
    allowed = (gap >= 0) & (gap < reach) & (key_pos < length) & (key_pos >= 0)
    return jnp.where(allowed, 0.0, NEG_FILL)


def pack_kernel(in_ref, out_ref):
    out_ref[0 : 2 * TOKENS, :] = in_ref[0 : 2 * TOKENS, :]
    low = in_ref[2 * TOKENS : 3 * TOKENS, RANK:].astype(jnp.float32)
    low = jnp.concatenate([low[:128], low[128:]], axis=1)
    out_ref[2 * TOKENS :, :] = low.astype(jnp.bfloat16)


def own_kernel(
    spot, both, pack, weight_ref, dprob_ref, stat_ref, g_ref, place, bias, score_buf
):
    def entry(at):
        return jnp.broadcast_to(spot[0:1, at : at + 1], (1, TOKENS))

    second = entry(1) == 1
    length = jnp.where(second, entry(3), entry(2))
    place[0:1, :] = entry(0)
    place[1:2, :] = length
    place[2:3, :] = jnp.where(second, entry(5), entry(4))
    token = lax.broadcasted_iota(jnp.int32, (TOKENS, HEAD_SIZE), 0)
    live = entry(0)[:, :HEAD_SIZE] * TOKENS + token < length[:, :HEAD_SIZE]
    live = jnp.where(live, 1.0, 0.0).astype(jnp.bfloat16)
    for head in range(HEADS):
        g_ref[:, lanes(head)] = both[TOKENS : 2 * TOKENS, lanes(head)] * live
    block_kernel(0, place, both, g_ref, pack, weight_ref, dprob_ref, stat_ref, bias, score_buf)


def block_kernel(
    stop, place, queries, cotangent, pack, weight_ref, dprob_ref, stat_ref, bias, score_buf
):
    bias[...] = visible_bias(place, stop)

    def products(head):
        score_buf[head % 2] = lax.dot_general(
            pack[0:TOKENS, :], queries[0:TOKENS, lanes(head)], NT, preferred_element_type=jnp.float32
        )
        dprob_ref[head] = lax.dot_general(
            pack[TOKENS : 2 * TOKENS, :],
            cotangent[:, lanes(head)],
            NT,
            preferred_element_type=jnp.float32,
        )

    products(0)
    for head in range(HEADS):
        if head + 1 < HEADS:
            products(head + 1)
        side = head % 2
        top = jnp.full((8, TOKENS), -3e38, jnp.float32)
        for rows in CHUNKS[: TOKENS // CHUNK]:
            scores = score_buf[side, rows] * (SCALE * LOG2E) + bias[rows]
            score_buf[side, rows] = scores
            top = jnp.maximum(top, jnp.max(folded(scores), axis=0))
        top = jnp.max(top, axis=0, keepdims=True)
        total = jnp.zeros((8, TOKENS), jnp.float32)
        inner = jnp.zeros((8, TOKENS), jnp.float32)
        for rows in CHUNKS[: TOKENS // CHUNK]:
            weights = jnp.exp2(score_buf[side, rows] - top)
            weight_ref[head, rows] = weights
            total = total + jnp.sum(folded(weights), axis=0)
            inner = inner + jnp.sum(folded(weights * dprob_ref[head, rows]), axis=0)
        stat_ref[head, 0:1, :] = top
        stat_ref[head, 1:2, :] = jnp.sum(total, axis=0, keepdims=True)
        stat_ref[head, 2:3, :] = jnp.sum(inner, axis=0, keepdims=True)


def attention_kernel(early_count, *refs):
    place, queries, cotangent, low_ref = refs[:4]
    packs = refs[4:8]
    early = [refs[8 + 3 * i : 11 + 3 * i] for i in range(early_count)]
    (
        keep_ref, send_ref, keys, values, keys_t, low_t, bias, sums,
        score_buf, dprob_buf, prob_buf, dscore_buf,
    ) = refs[8 + 3 * early_count :]
    core = place[0:1, :] % 2
    near = 1 + 2 * core
    first = core[:, :HEAD_SIZE] == 0
    stops = (0, 2, near, 4 - near)
    for slot in range(WINDOW_BLOCKS + 1):
        pack = packs[slot]
        rows = pl.ds(slot * TOKENS, TOKENS)
        key_block = pack[0:TOKENS, :]
        if slot >= early_count:
            fresh = pl.ds((slot - early_count) * TOKENS, TOKENS)
            keys[fresh, :] = key_block
            values[fresh, :] = pack[TOKENS : 2 * TOKENS, :]
            bias[fresh, :] = visible_bias(place, stops[slot])
        keys_t[:, rows] = key_block.T
        low_pair = pack[2 * TOKENS : PACK, :].T
        low_t[:, slot * TOKENS : slot * TOKENS + 128] = low_pair[:RANK]
        low_t[:, slot * TOKENS + 128 : (slot + 1) * TOKENS] = low_pair[RANK:]
    to = lax.broadcasted_iota(jnp.int32, (RANK, RANK), 0)
    source = lax.broadcasted_iota(jnp.int32, (RANK, RANK), 1)
    order = (to % 4) * 16 + (to % 32) // 4 * 2 + to // 32
    order = jnp.where(source == order, 1.0, 0.0).astype(jnp.bfloat16)
    query_low = low_ref[2 * TOKENS : 3 * TOKENS, :].T[:RANK]
    query_low = jnp.dot(order, query_low, preferred_element_type=jnp.float32).astype(jnp.bfloat16)
    value_low = jnp.dot(order, low_t[...], preferred_element_type=jnp.float32).astype(jnp.bfloat16)
    offset = early_count * TOKENS
    fresh_chunks = CHUNKS[: (KEYS - offset) // CHUNK]

    def products(head):
        side = head % 2
        score_buf[side] = lax.dot_general(
            keys[...], queries[0:TOKENS, lanes(head)], NT, preferred_element_type=jnp.float32
        )
        dprob_buf[side] = lax.dot_general(
            values[...], cotangent[:, lanes(head)], NT, preferred_element_type=jnp.float32
        )

    def softmax(head):
        side = head % 2
        top = jnp.full((8, TOKENS), -3e38, jnp.float32)
        for rows in fresh_chunks:
            scores = score_buf[side, rows] * (SCALE * LOG2E) + bias[rows]
            score_buf[side, rows] = scores
            top = jnp.maximum(top, jnp.max(folded(scores), axis=0))
        top = jnp.max(top, axis=0, keepdims=True)
        for _, _, stat in early:
            top = jnp.maximum(top, stat[head, 0:1, :])
        total = jnp.zeros((8, TOKENS), jnp.float32)
        inner = jnp.zeros((8, TOKENS), jnp.float32)
        for rows in fresh_chunks:
            weights = jnp.exp2(score_buf[side, rows] - top)
            score_buf[side, rows] = weights
            total = total + jnp.sum(folded(weights), axis=0)
            inner = inner + jnp.sum(folded(weights * dprob_buf[side, rows]), axis=0)
        total = jnp.sum(total, axis=0, keepdims=True)
        inner = jnp.sum(inner, axis=0, keepdims=True)
        fades = []
        for _, _, stat in early:
            fade = jnp.exp2(stat[head, 0:1, :] - top)
            total = total + fade * stat[head, 1:2, :]
            inner = inner + fade * stat[head, 2:3, :]
            fades.append(fade)
        fraction = 1.0 / total
        inner = inner * fraction

        def settle(weights, dprob, factor, at):
            prob = weights * factor
            prob_buf[side, at : at + CHUNK] = prob.astype(jnp.bfloat16)
            dscore_buf[side, at : at + CHUNK] = (prob * (dprob - inner)).astype(jnp.bfloat16)

        for slot, (weight, dprob, _) in enumerate(early):
            factor = fades[slot] * fraction
            for rows in CHUNKS[: TOKENS // CHUNK]:
                settle(weight[head, rows], dprob[head, rows], factor, slot * TOKENS + rows.start)
        for rows in fresh_chunks:
            settle(score_buf[side, rows], dprob_buf[side, rows], fraction, offset + rows.start)

    def finish(head, value_sum):
        side = head % 2
        query_grad = jnp.dot(keys_t[...], dscore_buf[side], preferred_element_type=jnp.float32)
        query_grad = (query_grad * SCALE).astype(jnp.bfloat16)
        sums[head] = lax.dot_general(
            query_low, query_grad, NT, preferred_element_type=jnp.float32
        )
        g = cotangent[:, lanes(head)]
        return value_sum + jnp.dot(prob_buf[side], g, preferred_element_type=jnp.float32)

    value_sum = jnp.zeros((KEYS, HEAD_SIZE), jnp.float32)
    products(0)
    for head in range(HEADS):
        if head + 1 < HEADS:
            products(head + 1)
        if head > 0:
            value_sum = finish(head - 1, value_sum)
        softmax(head)
    value_sum = finish(HEADS - 1, value_sum)
    sums[HEADS] = jnp.dot(
        value_low, value_sum.astype(jnp.bfloat16), preferred_element_type=jnp.float32
    )
    for head in range(HEADS + 1):
        even = sums[head, 0:32, :]
        odd = sums[head, 32:64, :]
        keep_ref[:, lanes(head)] = jnp.where(first, even, odd)
        send_ref[:, lanes(head)] = jnp.where(first, odd, even)


def pair_kernel(place, keep_ref, got_ref, out_ref):
    rows = RANK // 2
    first = jnp.broadcast_to(place[0:1, :128] % 2 == 0, (rows, 128))
    first = jnp.concatenate([first] * (FEATURES // 128), axis=1)
    total = keep_ref[...] + jnp.where(first, got_ref[rows:, :], got_ref[:rows, :])
    upper = jnp.concatenate([total[:, HALF:], jnp.zeros((32, 2 * HALF - FEATURES))], axis=1)
    both = jnp.stack([total[:, :HALF], upper], axis=1).astype(jnp.bfloat16)
    for seq in range(2):
        out_ref[:, seq] = both


def score_kernel(rows_ref, up_query, up_value, out_ref):
    pieces = []
    squares = []
    for b in range(2):
        row = jnp.sum(rows_ref[:, b].astype(jnp.float32), axis=0)
        row = jnp.concatenate([row[0:1], row[1:2, : FEATURES - HALF]], axis=1)
        squares.append(jnp.sum(row * row))
        total = up_value[...] * row[:, HEADS * HEAD_SIZE :]
        for k in range(HEADS):
            total = total + up_query[pl.ds(k, SHARE, stride=HEADS), :] * row[
                :, k * HEAD_SIZE : (k + 1) * HEAD_SIZE
            ]
        pieces.append(jnp.sum(total.T, axis=0, keepdims=True))
    lane = lax.broadcasted_iota(jnp.int32, (1, 128), 1)
    tail = jnp.where(lane == 0, squares[0], jnp.where(lane == 1, squares[1], 0.0))
    line = jnp.concatenate(pieces + [tail], axis=1)
    for i in range(out_ref.shape[0]):
        out_ref[i] = line


def relay_kernel(in_ref, out_ref):
    line = jnp.sum(in_ref[...], axis=0)
    for i in range(out_ref.shape[0]):
        out_ref[i] = line


def final_kernel(in_ref, ids_ref, out_ref):
    halves = [jnp.sum(in_ref[:, s], axis=0) for s in range(2)]
    count = 2 * SHARE
    rest = []
    for b in range(2):
        square = halves[0][:, count + b : count + b + 1]
        part = [half[:, b * SHARE : (b + 1) * SHARE] for half in halves]
        scores = jnp.concatenate(part, axis=1) / jnp.sqrt(square + 1e-06)
        rest.append(scores)
    slot = lax.broadcasted_iota(jnp.int32, (count, count), 0)
    chosen = jnp.where(slot == ids_ref[...], 1.0, 0.0).astype(jnp.bfloat16)
    left = jnp.concatenate(rest, axis=0)
    pieces = []
    for _ in range(3):
        piece = left.astype(jnp.bfloat16)
        left = left - piece.astype(jnp.float32)
        pieces.append(piece.astype(jnp.float32))
    pieces.append(jnp.zeros((2, count), jnp.float32))
    stack = jnp.concatenate(pieces, axis=0).astype(jnp.bfloat16)
    total = jnp.dot(stack, chosen, preferred_element_type=jnp.float32)
    out_ref[...] = total[0:2] + total[2:4] + total[4:6]


def call(kernel, made, specs, scratch=(), flops=0, out_specs=None):
    return pl.pallas_call(
        kernel,
        out_shape=[jax.ShapeDtypeStruct(*one) for one in made],
        in_specs=specs,
        out_specs=out_specs or [VMEM] * len(made),
        scratch_shapes=list(scratch),
        compiler_params=pltpu.CompilerParams(vmem_limit_bytes=32 * 2**20),
        cost_estimate=pl.CostEstimate(flops=flops, bytes_accessed=2**20, transcendentals=0),
    )


def body(
    queries, attention_keys, attention_values, cotangent, low_rank, seq_lengths,
    window_stops, query_ids, query_up_gradients, value_up_gradients,
):
    bf, f32 = jnp.bfloat16, jnp.float32
    three = jnp.concatenate([attention_keys[0], attention_values[0], low_rank[0]], axis=0)
    (pack,) = call(pack_kernel, [((PACK, HEAD_SIZE), bf)], [VMEM])(three)
    count = 64
    early = lax.ppermute(pack, CTX, [(i, i + 2) for i in range(count - 2)])
    apart = [(i, i + 1 + 2 * (i % 2)) for i in range(count) if i + 1 + 2 * (i % 2) < count]
    spot = jnp.stack([lax.axis_index(CTX), lax.axis_index("seq")]).astype(jnp.int32)
    spot = jnp.concatenate([spot, seq_lengths, window_stops])
    both = jnp.concatenate([queries[0], cotangent[0]], axis=0)
    later, both = lax.optimization_barrier((pack, both))
    far = lax.ppermute(later, CTX, apart)
    tile = (TOKENS, TOKENS)
    scored = [((HEADS, *tile), f32), ((HEADS, *tile), f32), ((HEADS, 8, TOKENS), f32)]
    scratch = [pltpu.VMEM(tile, f32), pltpu.VMEM((2, *tile), f32)]
    flops = 2 * 2 * HEADS * TOKENS * TOKENS * HEAD_SIZE
    row = ((TOKENS, HEADS * HEAD_SIZE), bf)
    *own, g, place = call(
        own_kernel, scored + [row, ((8, TOKENS), jnp.int32)],
        [VMEM] * 3, scratch, flops,
    )(spot.reshape(1, 6), both, pack)
    early, own[2] = lax.optimization_barrier((early, own[2]))
    other = lax.ppermute(early, "core", [(0, 1), (1, 0)])
    near = call(
        functools.partial(block_kernel, 2), scored, [VMEM] * 4, scratch, flops
    )(place, both, g, early)
    ready = [*own, *near]
    packs = [pack, early, other, far]
    fresh = KEYS - EARLY * TOKENS
    keep, send = call(
        functools.partial(attention_kernel, EARLY), [((RANK // 2, FEATURES), f32)] * 2,
        [VMEM] * (8 + 3 * EARLY),
        [
            pltpu.VMEM((fresh, HEAD_SIZE), bf),
            pltpu.VMEM((fresh, HEAD_SIZE), bf),
            pltpu.VMEM((HEAD_SIZE, KEYS), bf),
            pltpu.VMEM((RANK, KEYS), bf),
            pltpu.VMEM((fresh, TOKENS), f32),
            pltpu.VMEM((HEADS + 1, RANK, HEAD_SIZE), f32),
            pltpu.VMEM((2, fresh, TOKENS), f32),
            pltpu.VMEM((2, fresh, TOKENS), f32),
            pltpu.VMEM((2, KEYS, TOKENS), bf),
            pltpu.VMEM((2, KEYS, TOKENS), bf),
        ],
        flops=2 * 4 * HEADS * TOKENS * KEYS * HEAD_SIZE,
    )(place, both, g, three, *packs, *ready)
    got = lax.all_gather(send, "core", axis=0, tiled=True)
    (sums,) = call(pair_kernel, [((RANK // 2, 2, 2, HALF), bf)], [VMEM] * 3)(
        place, keep, got
    )
    sums = lax.all_to_all(sums.reshape(RANK, 2, HALF), ("z", "y", "seq"), 0, 0, tiled=True)
    up_query = query_up_gradients.reshape(SHARE * HEADS, HEAD_SIZE)
    up_value = value_up_gradients.reshape(SHARE, HEAD_SIZE)
    (lines,) = call(score_kernel, [((16, 1, LINE), f32)], [VMEM] * 3)(
        sums.reshape(RANK // 2, 2, 2, HALF), up_query, up_value
    )
    lines = lax.all_to_all(lines, ("z", "core"), 0, 0, tiled=True)
    (lines,) = call(relay_kernel, [((32, 1, LINE), f32)], [VMEM])(lines)
    lines = lax.all_to_all(lines, ("tp", "y", "seq"), 0, 0, tiled=True)
    (ranked,) = call(final_kernel, [((2, 2 * SHARE), f32)], [VMEM] * 2)(
        lines.reshape(16, 2, 1, LINE), query_ids.reshape(1, 2 * SHARE)
    )
    return ranked.T


def solution(mesh):
    fine = Mesh(mesh.devices.reshape(4, 8, 2, 4, 2), ("y", "z", "core", "tp", "seq"))
    split = P("seq", CTX, "tp")
    placed = (split, split, split, split, P("seq", CTX, None), P(), P(), P(), split, split)
    return jax.shard_map(body, mesh=fine, in_specs=placed, out_specs=P(), check_vma=False)
```

profile of v0, /device:TPU:1, one launch (start us, length us, event | category | flops | bytes accessed | tf_op | source)
XLA Modules:
  0.0 81.0 jit_solution(1832919136143569558)
XLA Ops:
  0.0 0.0 copy-start.3
  0.0 0.0 copy-start.4
  0.0 0.9 %pad_maximum_fusion.1.in_ref.refs_3_ = bf16[768,128]{1,0:T(8,128)(2,1)S(1)} fusion(bf16[256,128]{1,0:T(8,128)(2,1)} %bitcast.24, bf16[256,128]{1,0:T(8,128)(2,1)} %bitcast.25, bf16[256,128]{1,0:T(8,128)(2,1)} %bitcast.26), kind=kLoop, calls=%fused_computation.1 | loop fusion | flops 589824 | bytes 393216 | tf_op jit(solution)/shard_map/concatenate | solution.py:308
  0.9 0.1 shard_map.100.pack.refs_4_
  1.0 4.8 %collective-permute-start = (bf16[640,128]{1,0:T(8,128)(2,1)S(1)}, bf16[640,128]{1,0:T(8,128)(2,1)S(1)}, u32[]{:S(2)}, u32[]{:S(2)}) collective-permute-start(bf16[640,128]{1,0:T(8,128)(2,1)S(1)} %shard_map.100.pack.refs_4_), channel_id=1, source_target_pairs={{0,16},{8,24},{16,32},{24,40},{32,48},{40,56},{48,64},{56,72},{64,... | collective-permute-start | bytes 491528 | tf_op jit(solution)/shard_map/ppermute | solution.py:311
  5.9 1.3 %pad_maximum_fusion.both.queries.refs_1_ = bf16[512,1024]{1,0:T(8,128)(2,1)S(1)} fusion(bf16[256,1024]{1,0:T(8,128)(2,1)} %bitcast.22, bf16[256,1024]{1,0:T(8,128)(2,1)} %bitcast.23), kind=kLoop, calls=%fused_computation | loop fusion | flops 2097152 | bytes 2097152 | tf_op jit(solution)/shard_map/concatenate | solution.py:315
  7.1 6.6 %collective-permute-start.2 = (bf16[640,128]{1,0:T(8,128)(2,1)S(1)}, bf16[640,128]{1,0:T(8,128)(2,1)S(1)}, u32[]{:S(2)}, u32[]{:S(2)}) collective-permute-start(bf16[640,128]{1,0:T(8,128)(2,1)S(1)} %shard_map.100.pack.refs_4_), channel_id=1, source_target_pairs={{0,8},{8,32},{16,24},{24,48},{32,40},{40,64},{48,56},{56,80},{64,7... | collective-permute-start | bytes 491528 | tf_op jit(solution)/shard_map/ppermute | solution.py:317
  13.8 0.0 copy-done.3
  13.8 0.0 copy-done.4
  13.8 0.1 add_bitcast_fusion.spot
  13.9 1.2 %shard_map.101 = (f32[8,256,256]{2,1,0:T(8,128)S(1)}, f32[8,256,256]{2,1,0:T(8,128)S(1)}, f32[8,8,256]{2,1,0:T(8,128)S(1)}, bf16[256,1024]{1,0:T(8,128)(2,1)S(1)}, s32[8,256]{1,0:T(8,128)S(1)}) custom-call(s32[1,6]{1,0:T(1,128)S(1)} %add_bitcast_fusion.spot, bf16[512,1024]{1,0:T(8,128)(2,1)S(1)} %pad_maximum_fusion.both.queries.refs_1_, ...), custom_call_target="tpu_custom_call" | custom-call | flops 268435456 | bytes 1048576 | tf_op jit(solution)/shard_map/pallas_call | solution.py:323
  15.1 0.0 collective-permute-done.pack.refs_5_
  15.1 1.9 %collective-permute-start.1 = (bf16[640,128]{1,0:T(8,128)(2,1)S(1)}, bf16[640,128]{1,0:T(8,128)(2,1)S(1)}, u32[]{:S(2)}, u32[]{:S(2)}) collective-permute-start(bf16[640,128]{1,0:T(8,128)(2,1)S(1)} %collective-permute-done.pack.refs_5_), channel_id=1, source_target_pairs={{0,8},{8,0},{1,9},{9,1},{2,10},{10,2},{3,11},{11,3},{4,12},{12,4},... | collective-permute-start | bytes 491528 | tf_op jit(solution)/shard_map/ppermute | solution.py:328
  17.0 1.0 %shard_map.102 = (f32[8,256,256]{2,1,0:T(8,128)S(1)}, f32[8,256,256]{2,1,0:T(8,128)S(1)}, f32[8,8,256]{2,1,0:T(8,128)S(1)}) custom-call(s32[8,256]{1,0:T(8,128)S(1)} %get-tuple-element.20.place.refs_0_, bf16[512,1024]{1,0:T(8,128)(2,1)S(1)} %pad_maximum_fusion.both.queries.refs_1_, bf16[256,1024]{1,0:T(8,128)(2,1)S(1)} %get-tuple-element.21.cotangent.refs_2_, ...), custom_call_target="tpu_custom_call" | custom-call | flops 268435456 | bytes 1048576 | tf_op jit(solution)/shard_map/pallas_call | solution.py:329
  18.0 0.0 collective-permute-done.2.refs_7_
  18.0 0.4 collective-permute-done.1.refs_6_
  18.4 0.0 copy-start.1
  18.4 5.8 %shard_map.103 = (f32[32,1152]{1,0:T(8,128)S(1)}, f32[32,1152]{1,0:T(8,128)S(1)}) custom-call(s32[8,256]{1,0:T(8,128)S(1)} %get-tuple-element.20.place.refs_0_, bf16[512,1024]{1,0:T(8,128)(2,1)S(1)} %pad_maximum_fusion.both.queries.refs_1_, bf16[256,1024]{1,0:T(8,128)(2,1)S(1)} %get-tuple-element.21.cotangent.refs_2_, ...), custom_call_target="tpu_custom_call" | custom-call | flops 2147483648 | bytes 1048576 | tf_op jit(solution)/shard_map/pallas_call | solution.py:335
  24.1 0.0 copy-start
  24.2 0.0 copy-start.2
  24.2 2.1 %all_gather.3.got_ref = f32[64,1152]{1,0:T(8,128)S(1)} all-gather(f32[32,1152]{1,0:T(8,128)S(1)} %get-tuple-element.32), channel_id=1, replica_groups=mesh['y'=4,'z'=8,'core'=2,'tp'=4,'seq'=2] {'core'}, dimensions={0}, use_global_device_ids=true | all-gather | bytes 442368 | tf_op jit(solution)/shard_map/all_gather | solution.py:352
  26.3 0.2 shard_map.104
  26.5 27.5 %all_to_all.15 = bf16[64,2,640]{2,1,0:T(2,128)(2,1)S(1)} all-to-all(bf16[64,2,640]{2,1,0:T(2,128)(2,1)S(1)} %bitcast.17), channel_id=1, replica_groups=mesh['y'=4,'z'=8,'core'=2,'tp'=4,'seq'=2] {'z','y','seq'}, dimensions={0} | all-to-all | bytes 327680 | tf_op jit(solution)/shard_map/all_to_all | solution.py:356
  54.0 0.0 copy-done.1
  54.0 0.0 copy-done
  54.0 0.5 shard_map.105
  54.5 12.1 %all_to_all.16.in_ref = f32[16,1,640]{2,1,0:T(1,128)S(1)} all-to-all(f32[16,1,640]{2,1,0:T(1,128)S(1)} %shard_map.105), channel_id=1, replica_groups=mesh['y'=4,'z'=8,'core'=2,'tp'=4,'seq'=2] {'z','core'}, dimensions={0} | all-to-all | bytes 81920 | tf_op jit(solution)/shard_map/all_to_all | solution.py:362
  66.6 13.5 %all_to_all.17 = f32[32,1,640]{2,1,0:T(1,128)S(1)} all-to-all(f32[32,1,640]{2,1,0:T(1,128)S(1)} %shard_map.106), channel_id=1, replica_groups=mesh['y'=4,'z'=8,'core'=2,'tp'=4,'seq'=2] {'tp','y','seq'}, dimensions={0} | all-to-all | bytes 163840 | tf_op jit(solution)/shard_map/all_to_all | solution.py:364
  80.1 0.0 copy-done.2
  80.1 0.9 %shard_map.107 = f32[2,512]{1,0:T(2,128)} custom-call(f32[16,2,1,640]{3,2,1,0:T(1,128)S(1)} %bitcast.19, s32[1,512]{1,0:T(1,128)S(1)} %bitcast.21), custom_call_target="tpu_custom_call" | custom-call | bytes 1048576 | tf_op jit(solution)/shard_map/pallas_call | solution.py:365
  (1 shorter events, 0.0 us)
Async XLA Ops:
  0.0 13.8 %copy-start.3 = (s32[2]{0:T(128)S(1)}, s32[2]{0:T(128)}, u32[]{:S(2)}) copy-start(s32[2]{0:T(128)} %param.16) | copy-start | bytes 28
  0.0 13.8 %copy-start.4 = (s32[2]{0:T(128)S(1)}, s32[2]{0:T(128)}, u32[]{:S(2)}) copy-start(s32[2]{0:T(128)} %param.15) | copy-start | bytes 28
  1.0 14.0 %collective-permute-start = (bf16[640,128]{1,0:T(8,128)(2,1)S(1)}, bf16[640,128]{1,0:T(8,128)(2,1)S(1)}, u32[]{:S(2)}, u32[]{:S(2)}) collective-permute-start(bf16[640,128]{1,0:T(8,128)(2,1)S(1)} %shard_map.100.pack.refs_4_), channel_id=1, source_target_pairs={{0,16},{8,24},{16,32},{24,40},{32,48},{40,56},{48,64},{56,72},{64,... | collective-permute-start | bytes 491528 | tf_op jit(solution)/shard_map/ppermute | solution.py:311
  7.1 10.9 %collective-permute-start.2 = (bf16[640,128]{1,0:T(8,128)(2,1)S(1)}, bf16[640,128]{1,0:T(8,128)(2,1)S(1)}, u32[]{:S(2)}, u32[]{:S(2)}) collective-permute-start(bf16[640,128]{1,0:T(8,128)(2,1)S(1)} %shard_map.100.pack.refs_4_), channel_id=1, source_target_pairs={{0,8},{8,32},{16,24},{24,48},{32,40},{40,64},{48,56},{56,80},{64,7... | collective-permute-start | bytes 491528 | tf_op jit(solution)/shard_map/ppermute | solution.py:317
  15.1 3.3 %collective-permute-start.1 = (bf16[640,128]{1,0:T(8,128)(2,1)S(1)}, bf16[640,128]{1,0:T(8,128)(2,1)S(1)}, u32[]{:S(2)}, u32[]{:S(2)}) collective-permute-start(bf16[640,128]{1,0:T(8,128)(2,1)S(1)} %collective-permute-done.pack.refs_5_), channel_id=1, source_target_pairs={{0,8},{8,0},{1,9},{9,1},{2,10},{10,2},{3,11},{11,3},{4,12},{12,4},... | collective-permute-start | bytes 491528 | tf_op jit(solution)/shard_map/ppermute | solution.py:328
  18.4 35.6 %copy-start.1 = (f32[256,1,128]{2,1,0:T(1,128)S(1)}, f32[256,1,128]{2,1,0:T(1,128)}, u32[]{:S(2)}) copy-start(f32[256,1,128]{2,1,0:T(1,128)} %param.19) | copy-start | bytes 393220
  24.1 29.8 %copy-start = (f32[256,1,1024]{2,1,0:T(1,128)S(1)}, f32[256,1,1024]{2,1,0:T(1,128)}, u32[]{:S(2)}) copy-start(f32[256,1,1024]{2,1,0:T(1,128)} %param.18) | copy-start | bytes 3145732
  24.2 56.0 %copy-start.2 = (s32[512]{0:T(512)S(1)}, s32[512]{0:T(512)}, u32[]{:S(2)}) copy-start(s32[512]{0:T(512)} %param.17) | copy-start | bytes 6148
where the time goes:
time: 81.3 us; the launch traced here: 81 us
  blocking collectives  55.2 us (68%)
  starting transfers between devices  13.4 us (16%)
  Pallas kernels  9.6 us (12%)
  other arithmetic  2.29 us (3%)
    all_to_all x1, blocking collectives, body(): lax.all_to_all(sums.reshape(RANK, 2, HALF), ('z', 'y', 'seq'), 0, 0, tile...  27.5 us
    all_to_all x1, blocking collectives, body(): lines = lax.all_to_all(lines, ('tp', 'y', 'seq'), 0, 0, tiled=True)  13.5 us
    all_to_all x1, blocking collectives, body(): lines = lax.all_to_all(lines, ('z', 'core'), 0, 0, tiled=True)  12.1 us
    ppermute x1, starting transfers between devices, body(): far = lax.ppermute(later, CTX, apart)  6.64 us
    pallas_call x1, Pallas kernels, body(): call(functools.partial(attention_kernel, EARLY), [((RANK // 2, FEATURES),...  5.77 us
    ppermute x1, starting transfers between devices, body(): early = lax.ppermute(pack, CTX, [(i, i + 2) for i in range(count - 2)])  4.82 us
    all_gather x1, blocking collectives, body(): got = lax.all_gather(send, 'core', axis=0, tiled=True)  2.15 us
    ppermute x1, starting transfers between devices, body(): other = lax.ppermute(early, 'core', [(0, 1), (1, 0)])  1.92 us
  transfers between devices with their start and end apart: 3, of which 1 were waited for; matrix products, arithmetic and copies ran while one was open for 2% of the time, Pallas kernels for 3%

commit v1 on v0

--- a/solution.py
+++ b/solution.py
@@ -57,9 +57,27 @@
     out_ref[2 * TOKENS :, :] = low.astype(jnp.bfloat16)
 
 
-def own_kernel(
-    spot, both, pack, weight_ref, dprob_ref, stat_ref, g_ref, place, bias, score_buf
-):
+def row_order():
+    to = lax.broadcasted_iota(jnp.int32, (RANK, RANK), 0)
+    source = lax.broadcasted_iota(jnp.int32, (RANK, RANK), 1)
+    order = (to % 4) * 16 + (to % 32) // 4 * 2 + to // 32
+    return jnp.where(source == order, 1.0, 0.0).astype(jnp.bfloat16)
+
+
+def ordered(low):
+    low = jnp.dot(row_order(), low, preferred_element_type=jnp.float32)
+    return low.astype(jnp.bfloat16)
+
+
+def value_low(pack):
+    low = pack[2 * TOKENS : PACK, :].T
+    return ordered(jnp.concatenate([low[:RANK], low[RANK:]], axis=1))
+
+
+def own_kernel(spot, both, pack, low_ref, *refs):
+    g_ref, place, query_low = refs[5:8]
+    query_low[...] = ordered(low_ref[2 * TOKENS : 3 * TOKENS, :].T[:RANK])
+
     def entry(at):
         return jnp.broadcast_to(spot[0:1, at : at + 1], (1, TOKENS))
 
@@ -73,13 +91,16 @@
     live = jnp.where(live, 1.0, 0.0).astype(jnp.bfloat16)
     for head in range(HEADS):
         g_ref[:, lanes(head)] = both[TOKENS : 2 * TOKENS, lanes(head)] * live
-    block_kernel(0, place, both, g_ref, pack, weight_ref, dprob_ref, stat_ref, bias, score_buf)
+    block_kernel(0, place, both, g_ref, pack, *refs[:5], *refs[8:])
 
 
 def block_kernel(
-    stop, place, queries, cotangent, pack, weight_ref, dprob_ref, stat_ref, bias, score_buf
+    stop, place, queries, cotangent, pack,
+    weight_ref, dprob_ref, stat_ref, key_t, low_t, bias, score_buf,
 ):
     bias[...] = visible_bias(place, stop)
+    key_t[...] = pack[0:TOKENS, :].T
+    low_t[...] = value_low(pack)
 
     def products(head):
         score_buf[head % 2] = lax.dot_general(
@@ -116,13 +137,13 @@
 
 
 def attention_kernel(early_count, *refs):
-    place, queries, cotangent, low_ref = refs[:4]
+    place, queries, cotangent, query_low = refs[:4]
     packs = refs[4:8]
-    early = [refs[8 + 3 * i : 11 + 3 * i] for i in range(early_count)]
+    early = [refs[8 + 5 * i : 13 + 5 * i] for i in range(early_count)]
     (
         keep_ref, send_ref, keys, values, keys_t, low_t, bias, sums,
         score_buf, dprob_buf, prob_buf, dscore_buf,
-    ) = refs[8 + 3 * early_count :]
+    ) = refs[8 + 5 * early_count :]
     core = place[0:1, :] % 2
     near = 1 + 2 * core
     first = core[:, :HEAD_SIZE] == 0
@@ -130,23 +151,17 @@
     for slot in range(WINDOW_BLOCKS + 1):
         pack = packs[slot]
         rows = pl.ds(slot * TOKENS, TOKENS)
-        key_block = pack[0:TOKENS, :]
-        if slot >= early_count:
+        if slot < early_count:
+            keys_t[:, rows] = early[slot][3][...]
+            low_t[:, rows] = early[slot][4][...]
+        else:
+            key_block = pack[0:TOKENS, :]
             fresh = pl.ds((slot - early_count) * TOKENS, TOKENS)
             keys[fresh, :] = key_block
             values[fresh, :] = pack[TOKENS : 2 * TOKENS, :]
             bias[fresh, :] = visible_bias(place, stops[slot])
-        keys_t[:, rows] = key_block.T
-        low_pair = pack[2 * TOKENS : PACK, :].T
-        low_t[:, slot * TOKENS : slot * TOKENS + 128] = low_pair[:RANK]
-        low_t[:, slot * TOKENS + 128 : (slot + 1) * TOKENS] = low_pair[RANK:]
-    to = lax.broadcasted_iota(jnp.int32, (RANK, RANK), 0)
-    source = lax.broadcasted_iota(jnp.int32, (RANK, RANK), 1)
-    order = (to % 4) * 16 + (to % 32) // 4 * 2 + to // 32
-    order = jnp.where(source == order, 1.0, 0.0).astype(jnp.bfloat16)
-    query_low = low_ref[2 * TOKENS : 3 * TOKENS, :].T[:RANK]
-    query_low = jnp.dot(order, query_low, preferred_element_type=jnp.float32).astype(jnp.bfloat16)
-    value_low = jnp.dot(order, low_t[...], preferred_element_type=jnp.float32).astype(jnp.bfloat16)
+            keys_t[:, rows] = key_block.T
+            low_t[:, rows] = value_low(pack)
     offset = early_count * TOKENS
     fresh_chunks = CHUNKS[: (KEYS - offset) // CHUNK]
 
@@ -167,7 +182,7 @@
             score_buf[side, rows] = scores
             top = jnp.maximum(top, jnp.max(folded(scores), axis=0))
         top = jnp.max(top, axis=0, keepdims=True)
-        for _, _, stat in early:
+        for _, _, stat, _, _ in early:
             top = jnp.maximum(top, stat[head, 0:1, :])
         total = jnp.zeros((8, TOKENS), jnp.float32)
         inner = jnp.zeros((8, TOKENS), jnp.float32)
@@ -179,7 +194,7 @@
         total = jnp.sum(total, axis=0, keepdims=True)
         inner = jnp.sum(inner, axis=0, keepdims=True)
         fades = []
-        for _, _, stat in early:
+        for _, _, stat, _, _ in early:
             fade = jnp.exp2(stat[head, 0:1, :] - top)
             total = total + fade * stat[head, 1:2, :]
             inner = inner + fade * stat[head, 2:3, :]
@@ -192,7 +207,7 @@
             prob_buf[side, at : at + CHUNK] = prob.astype(jnp.bfloat16)
             dscore_buf[side, at : at + CHUNK] = (prob * (dprob - inner)).astype(jnp.bfloat16)
 
-        for slot, (weight, dprob, _) in enumerate(early):
+        for slot, (weight, dprob, *_) in enumerate(early):
             factor = fades[slot] * fraction
             for rows in CHUNKS[: TOKENS // CHUNK]:
                 settle(weight[head, rows], dprob[head, rows], factor, slot * TOKENS + rows.start)
@@ -204,7 +219,7 @@
         query_grad = jnp.dot(keys_t[...], dscore_buf[side], preferred_element_type=jnp.float32)
         query_grad = (query_grad * SCALE).astype(jnp.bfloat16)
         sums[head] = lax.dot_general(
-            query_low, query_grad, NT, preferred_element_type=jnp.float32
+            query_low[...], query_grad, NT, preferred_element_type=jnp.float32
         )
         g = cotangent[:, lanes(head)]
         return value_sum + jnp.dot(prob_buf[side], g, preferred_element_type=jnp.float32)
@@ -219,7 +234,7 @@
         softmax(head)
     value_sum = finish(HEADS - 1, value_sum)
     sums[HEADS] = jnp.dot(
-        value_low, value_sum.astype(jnp.bfloat16), preferred_element_type=jnp.float32
+        low_t[...], value_sum.astype(jnp.bfloat16), preferred_element_type=jnp.float32
     )
     for head in range(HEADS + 1):
         even = sums[head, 0:32, :]
@@ -317,13 +332,14 @@
     far = lax.ppermute(later, CTX, apart)
     tile = (TOKENS, TOKENS)
     scored = [((HEADS, *tile), f32), ((HEADS, *tile), f32), ((HEADS, 8, TOKENS), f32)]
+    scored += [((HEAD_SIZE, TOKENS), bf), ((RANK, TOKENS), bf)]
     scratch = [pltpu.VMEM(tile, f32), pltpu.VMEM((2, *tile), f32)]
     flops = 2 * 2 * HEADS * TOKENS * TOKENS * HEAD_SIZE
     row = ((TOKENS, HEADS * HEAD_SIZE), bf)
-    *own, g, place = call(
-        own_kernel, scored + [row, ((8, TOKENS), jnp.int32)],
-        [VMEM] * 3, scratch, flops,
-    )(spot.reshape(1, 6), both, pack)
+    *own, g, place, turned = call(
+        own_kernel, scored + [row, ((8, TOKENS), jnp.int32), ((RANK, TOKENS), bf)],
+        [VMEM] * 4, scratch, flops,
+    )(spot.reshape(1, 6), both, pack, three)
     early, own[2] = lax.optimization_barrier((early, own[2]))
     other = lax.ppermute(early, "core", [(0, 1), (1, 0)])
     near = call(
@@ -334,7 +350,7 @@
     fresh = KEYS - EARLY * TOKENS
     keep, send = call(
         functools.partial(attention_kernel, EARLY), [((RANK // 2, FEATURES), f32)] * 2,
-        [VMEM] * (8 + 3 * EARLY),
+        [VMEM] * (8 + 5 * EARLY),
         [
             pltpu.VMEM((fresh, HEAD_SIZE), bf),
             pltpu.VMEM((fresh, HEAD_SIZE), bf),
@@ -348,7 +364,7 @@
             pltpu.VMEM((2, KEYS, TOKENS), bf),
         ],
         flops=2 * 4 * HEADS * TOKENS * KEYS * HEAD_SIZE,
-    )(place, both, g, three, *packs, *ready)
+    )(place, both, g, turned, *packs, *ready)
     got = lax.all_gather(send, "core", axis=0, tiled=True)
     (sums,) = call(pair_kernel, [((RANK // 2, 2, 2, HALF), bf)], [VMEM] * 3)(
         place, keep, got

time: 81.3 us -> 81.4 us (level)
  no operation moved by 1% of the time
where the time goes in v1:
time: 81.4 us; the launch traced here: 81 us
  blocking collectives  55.1 us (68%)
  starting transfers between devices  13.4 us (16%)
  Pallas kernels  9.79 us (12%)
  other arithmetic  2.29 us (3%)
    all_to_all x1, blocking collectives, body(): lax.all_to_all(sums.reshape(RANK, 2, HALF), ('z', 'y', 'seq'), 0, 0, tile...  27.4 us
    all_to_all x1, blocking collectives, body(): lines = lax.all_to_all(lines, ('tp', 'y', 'seq'), 0, 0, tiled=True)  13.5 us
    all_to_all x1, blocking collectives, body(): lines = lax.all_to_all(lines, ('z', 'core'), 0, 0, tiled=True)  12.1 us
    ppermute x1, starting transfers between devices, body(): far = lax.ppermute(later, CTX, apart)  6.64 us
    pallas_call x1, Pallas kernels, body(): call(functools.partial(attention_kernel, EARLY), [((RANK // 2, FEATURES),...  5.82 us
    ppermute x1, starting transfers between devices, body(): early = lax.ppermute(pack, CTX, [(i, i + 2) for i in range(count - 2)])  4.82 us
    all_gather x1, blocking collectives, body(): got = lax.all_gather(send, 'core', axis=0, tiled=True)  2.15 us
    ppermute x1, starting transfers between devices, body(): other = lax.ppermute(early, 'core', [(0, 1), (1, 0)])  1.92 us
  transfers between devices with their start and end apart: 3, of which 1 were waited for; matrix products, arithmetic and copies ran while one was open for 2% of the time, Pallas kernels for 3%

profile of v1, /device:TPU:1, one launch (start us, length us, event | category | flops | bytes accessed | tf_op | source)
XLA Modules:
  0.0 81.0 jit_solution(7329061351685725303)
XLA Ops:
  0.0 0.0 copy-start.3
  0.0 0.0 copy-start.4
  0.0 0.9 %pad_maximum_fusion.1.in_ref.low_ref = bf16[768,128]{1,0:T(8,128)(2,1)S(1)} fusion(bf16[256,128]{1,0:T(8,128)(2,1)} %bitcast.24, bf16[256,128]{1,0:T(8,128)(2,1)} %bitcast.25, bf16[256,128]{1,0:T(8,128)(2,1)} %bitcast.26), kind=kLoop, calls=%fused_computation.1 | loop fusion | flops 589824 | bytes 393216 | tf_op jit(solution)/shard_map/concatenate | solution.py:323
  0.9 0.1 shard_map.100.pack.refs_4_
  1.0 4.8 %collective-permute-start = (bf16[640,128]{1,0:T(8,128)(2,1)S(1)}, bf16[640,128]{1,0:T(8,128)(2,1)S(1)}, u32[]{:S(2)}, u32[]{:S(2)}) collective-permute-start(bf16[640,128]{1,0:T(8,128)(2,1)S(1)} %shard_map.100.pack.refs_4_), channel_id=1, source_target_pairs={{0,16},{8,24},{16,32},{24,40},{32,48},{40,56},{48,64},{56,72},{64,... | collective-permute-start | bytes 491528 | tf_op jit(solution)/shard_map/ppermute | solution.py:326
  5.9 1.3 %pad_maximum_fusion.both.queries.refs_1_ = bf16[512,1024]{1,0:T(8,128)(2,1)S(1)} fusion(bf16[256,1024]{1,0:T(8,128)(2,1)} %bitcast.22, bf16[256,1024]{1,0:T(8,128)(2,1)} %bitcast.23), kind=kLoop, calls=%fused_computation | loop fusion | flops 2097152 | bytes 2097152 | tf_op jit(solution)/shard_map/concatenate | solution.py:330
  7.1 6.6 %collective-permute-start.2 = (bf16[640,128]{1,0:T(8,128)(2,1)S(1)}, bf16[640,128]{1,0:T(8,128)(2,1)S(1)}, u32[]{:S(2)}, u32[]{:S(2)}) collective-permute-start(bf16[640,128]{1,0:T(8,128)(2,1)S(1)} %shard_map.100.pack.refs_4_), channel_id=1, source_target_pairs={{0,8},{8,32},{16,24},{24,48},{32,40},{40,64},{48,56},{56,80},{64,7... | collective-permute-start | bytes 491528 | tf_op jit(solution)/shard_map/ppermute | solution.py:332
  13.8 0.0 copy-done.3
  13.8 0.0 copy-done.4
  13.8 0.1 add_bitcast_fusion.spot
  13.9 1.2 %shard_map.101 = (f32[8,256,256]{2,1,0:T(8,128)S(1)}, f32[8,256,256]{2,1,0:T(8,128)S(1)}, f32[8,8,256]{2,1,0:T(8,128)S(1)}, bf16[128,256]{1,0:T(8,128)(2,1)S(1)}...) custom-call(s32[1,6]{1,0:T(1,128)S(1)} %add_bitcast_fusion.spot, ...), custom_call_target="tpu_custom_call" | custom-call | flops 268435456 | bytes 1048576 | tf_op jit(solution)/shard_map/pallas_call | solution.py:339
  15.1 0.0 collective-permute-done.pack.refs_5_
  15.2 1.9 %collective-permute-start.1 = (bf16[640,128]{1,0:T(8,128)(2,1)S(1)}, bf16[640,128]{1,0:T(8,128)(2,1)S(1)}, u32[]{:S(2)}, u32[]{:S(2)}) collective-permute-start(bf16[640,128]{1,0:T(8,128)(2,1)S(1)} %collective-permute-done.pack.refs_5_), channel_id=1, source_target_pairs={{0,8},{8,0},{1,9},{9,1},{2,10},{10,2},{3,11},{11,3},{4,12},{12,4},... | collective-permute-start | bytes 491528 | tf_op jit(solution)/shard_map/ppermute | solution.py:344
  17.1 1.1 %shard_map.102 = (f32[8,256,256]{2,1,0:T(8,128)S(1)}, f32[8,256,256]{2,1,0:T(8,128)S(1)}, f32[8,8,256]{2,1,0:T(8,128)S(1)}, bf16[128,256]{1,0:T(8,128)(2,1)S(1)}, bf16[64,256]{1,0:T(8,128)(2,1)S(1)}) custom-call(s32[8,256]{1,0:T(8,128)S(1)} %get-tuple-element.25.place.refs_0_, bf16[512,1024]{1,0:T(8,128)(2,1)S(1)} %pad_maximum_fusion.both.queries.refs_1_, ...), custom_call_target="tpu_custom_call" | custom-call | flops 268435456 | bytes 1048576 | tf_op jit(solution)/shard_map/pallas_call | solution.py:345
  18.1 0.0 collective-permute-done.2.refs_7_
  18.1 0.3 collective-permute-done.1.refs_6_
  18.4 0.0 copy-start.1
  18.4 5.8 %shard_map.103 = (f32[32,1152]{1,0:T(8,128)S(1)}, f32[32,1152]{1,0:T(8,128)S(1)}) custom-call(s32[8,256]{1,0:T(8,128)S(1)} %get-tuple-element.25.place.refs_0_, bf16[512,1024]{1,0:T(8,128)(2,1)S(1)} %pad_maximum_fusion.both.queries.refs_1_, bf16[256,1024]{1,0:T(8,128)(2,1)S(1)} %get-tuple-element.26.cotangent.refs_2_, ...), custom_call_target="tpu_custom_call" | custom-call | flops 2147483648 | bytes 1048576 | tf_op jit(solution)/shard_map/pallas_call | solution.py:351
  24.3 0.0 copy-start
  24.3 0.0 copy-start.2
  24.3 2.1 %all_gather.3.got_ref = f32[64,1152]{1,0:T(8,128)S(1)} all-gather(f32[32,1152]{1,0:T(8,128)S(1)} %get-tuple-element.42), channel_id=1, replica_groups=mesh['y'=4,'z'=8,'core'=2,'tp'=4,'seq'=2] {'core'}, dimensions={0}, use_global_device_ids=true | all-gather | bytes 442368 | tf_op jit(solution)/shard_map/all_gather | solution.py:368
  26.4 0.2 shard_map.104
  26.6 27.4 %all_to_all.15 = bf16[64,2,640]{2,1,0:T(2,128)(2,1)S(1)} all-to-all(bf16[64,2,640]{2,1,0:T(2,128)(2,1)S(1)} %bitcast.17), channel_id=1, replica_groups=mesh['y'=4,'z'=8,'core'=2,'tp'=4,'seq'=2] {'z','y','seq'}, dimensions={0} | all-to-all | bytes 327680 | tf_op jit(solution)/shard_map/all_to_all | solution.py:372
  54.0 0.0 copy-done.1
  54.0 0.0 copy-done
  54.0 0.5 shard_map.105
  54.6 12.1 %all_to_all.16.in_ref = f32[16,1,640]{2,1,0:T(1,128)S(1)} all-to-all(f32[16,1,640]{2,1,0:T(1,128)S(1)} %shard_map.105), channel_id=1, replica_groups=mesh['y'=4,'z'=8,'core'=2,'tp'=4,'seq'=2] {'z','core'}, dimensions={0} | all-to-all | bytes 81920 | tf_op jit(solution)/shard_map/all_to_all | solution.py:378
  66.7 13.5 %all_to_all.17 = f32[32,1,640]{2,1,0:T(1,128)S(1)} all-to-all(f32[32,1,640]{2,1,0:T(1,128)S(1)} %shard_map.106), channel_id=1, replica_groups=mesh['y'=4,'z'=8,'core'=2,'tp'=4,'seq'=2] {'tp','y','seq'}, dimensions={0} | all-to-all | bytes 163840 | tf_op jit(solution)/shard_map/all_to_all | solution.py:380
  80.2 0.0 copy-done.2
  80.2 0.9 %shard_map.107 = f32[2,512]{1,0:T(2,128)} custom-call(f32[16,2,1,640]{3,2,1,0:T(1,128)S(1)} %bitcast.19, s32[1,512]{1,0:T(1,128)S(1)} %bitcast.21), custom_call_target="tpu_custom_call" | custom-call | bytes 1048576 | tf_op jit(solution)/shard_map/pallas_call | solution.py:381
  (1 shorter events, 0.0 us)
Async XLA Ops:
  0.0 13.8 %copy-start.3 = (s32[2]{0:T(128)S(1)}, s32[2]{0:T(128)}, u32[]{:S(2)}) copy-start(s32[2]{0:T(128)} %param.16) | copy-start | bytes 28
  0.0 13.8 %copy-start.4 = (s32[2]{0:T(128)S(1)}, s32[2]{0:T(128)}, u32[]{:S(2)}) copy-start(s32[2]{0:T(128)} %param.15) | copy-start | bytes 28
  1.0 14.1 %collective-permute-start = (bf16[640,128]{1,0:T(8,128)(2,1)S(1)}, bf16[640,128]{1,0:T(8,128)(2,1)S(1)}, u32[]{:S(2)}, u32[]{:S(2)}) collective-permute-start(bf16[640,128]{1,0:T(8,128)(2,1)S(1)} %shard_map.100.pack.refs_4_), channel_id=1, source_target_pairs={{0,16},{8,24},{16,32},{24,40},{32,48},{40,56},{48,64},{56,72},{64,... | collective-permute-start | bytes 491528 | tf_op jit(solution)/shard_map/ppermute | solution.py:326
  7.1 11.0 %collective-permute-start.2 = (bf16[640,128]{1,0:T(8,128)(2,1)S(1)}, bf16[640,128]{1,0:T(8,128)(2,1)S(1)}, u32[]{:S(2)}, u32[]{:S(2)}) collective-permute-start(bf16[640,128]{1,0:T(8,128)(2,1)S(1)} %shard_map.100.pack.refs_4_), channel_id=1, source_target_pairs={{0,8},{8,32},{16,24},{24,48},{32,40},{40,64},{48,56},{56,80},{64,7... | collective-permute-start | bytes 491528 | tf_op jit(solution)/shard_map/ppermute | solution.py:332
  15.2 3.3 %collective-permute-start.1 = (bf16[640,128]{1,0:T(8,128)(2,1)S(1)}, bf16[640,128]{1,0:T(8,128)(2,1)S(1)}, u32[]{:S(2)}, u32[]{:S(2)}) collective-permute-start(bf16[640,128]{1,0:T(8,128)(2,1)S(1)} %collective-permute-done.pack.refs_5_), channel_id=1, source_target_pairs={{0,8},{8,0},{1,9},{9,1},{2,10},{10,2},{3,11},{11,3},{4,12},{12,4},... | collective-permute-start | bytes 491528 | tf_op jit(solution)/shard_map/ppermute | solution.py:344
  18.4 35.6 %copy-start.1 = (f32[256,1,128]{2,1,0:T(1,128)S(1)}, f32[256,1,128]{2,1,0:T(1,128)}, u32[]{:S(2)}) copy-start(f32[256,1,128]{2,1,0:T(1,128)} %param.19) | copy-start | bytes 393220
  24.3 29.8 %copy-start = (f32[256,1,1024]{2,1,0:T(1,128)S(1)}, f32[256,1,1024]{2,1,0:T(1,128)}, u32[]{:S(2)}) copy-start(f32[256,1,1024]{2,1,0:T(1,128)} %param.18) | copy-start | bytes 3145732
  24.3 55.9 %copy-start.2 = (s32[512]{0:T(512)S(1)}, s32[512]{0:T(512)}, u32[]{:S(2)}) copy-start(s32[512]{0:T(512)} %param.17) | copy-start | bytes 6148

commit v2 on v0

--- a/solution.py
+++ b/solution.py
@@ -225,14 +225,15 @@
         even = sums[head, 0:32, :]
         odd = sums[head, 32:64, :]
         keep_ref[:, lanes(head)] = jnp.where(first, even, odd)
-        send_ref[:, lanes(head)] = jnp.where(first, odd, even)
+        send_ref[:, lanes(head)] = jnp.where(first, odd, even).astype(jnp.bfloat16)
 
 
 def pair_kernel(place, keep_ref, got_ref, out_ref):
     rows = RANK // 2
     first = jnp.broadcast_to(place[0:1, :128] % 2 == 0, (rows, 128))
     first = jnp.concatenate([first] * (FEATURES // 128), axis=1)
-    total = keep_ref[...] + jnp.where(first, got_ref[rows:, :], got_ref[:rows, :])
+    got = got_ref[...].astype(jnp.float32)
+    total = keep_ref[...] + jnp.where(first, got[rows:], got[:rows])
     upper = jnp.concatenate([total[:, HALF:], jnp.zeros((32, 2 * HALF - FEATURES))], axis=1)
     both = jnp.stack([total[:, :HALF], upper], axis=1).astype(jnp.bfloat16)
     for seq in range(2):
@@ -333,7 +334,7 @@
     packs = [pack, early, other, far]
     fresh = KEYS - EARLY * TOKENS
     keep, send = call(
-        functools.partial(attention_kernel, EARLY), [((RANK // 2, FEATURES), f32)] * 2,
+        functools.partial(attention_kernel, EARLY), [((RANK // 2, FEATURES), f32), ((RANK // 2, FEATURES), bf)],
         [VMEM] * (8 + 3 * EARLY),
         [
             pltpu.VMEM((fresh, HEAD_SIZE), bf),

time: 81.3 us -> 81 us (level)
  no operation moved by 1% of the time
where the time goes in v2:
time: 81 us; the launch traced here: 80.7 us
  blocking collectives  55 us (68%)
  starting transfers between devices  13.4 us (17%)
  Pallas kernels  9.5 us (12%)
  other arithmetic  2.29 us (3%)
    all_to_all x1, blocking collectives, body(): lax.all_to_all(sums.reshape(RANK, 2, HALF), ('z', 'y', 'seq'), 0, 0, tile...  27.5 us
    all_to_all x1, blocking collectives, body(): lines = lax.all_to_all(lines, ('tp', 'y', 'seq'), 0, 0, tiled=True)  13.5 us
    all_to_all x1, blocking collectives, body(): lines = lax.all_to_all(lines, ('z', 'core'), 0, 0, tiled=True)  12.1 us
    ppermute x1, starting transfers between devices, body(): far = lax.ppermute(later, CTX, apart)  6.64 us
    pallas_call x1, Pallas kernels, body(): call(functools.partial(attention_kernel, EARLY), [((RANK // 2, FEATURES),...  5.68 us
    ppermute x1, starting transfers between devices, body(): early = lax.ppermute(pack, CTX, [(i, i + 2) for i in range(count - 2)])  4.82 us
    ppermute x1, starting transfers between devices, body(): other = lax.ppermute(early, 'core', [(0, 1), (1, 0)])  1.92 us
    all_gather x1, blocking collectives, body(): got = lax.all_gather(send, 'core', axis=0, tiled=True)  1.91 us
  transfers between devices with their start and end apart: 3, of which 1 were waited for; matrix products, arithmetic and copies ran while one was open for 2% of the time, Pallas kernels for 3%

profile of v2, /device:TPU:1, one launch (start us, length us, event | category | flops | bytes accessed | tf_op | source)
XLA Modules:
  0.0 80.7 jit_solution(16797110689212250323)
XLA Ops:
  0.0 0.0 copy-start.3
  0.0 0.0 copy-start.4
  0.0 0.9 %pad_maximum_fusion.1.in_ref.refs_3_ = bf16[768,128]{1,0:T(8,128)(2,1)S(1)} fusion(bf16[256,128]{1,0:T(8,128)(2,1)} %bitcast.24, bf16[256,128]{1,0:T(8,128)(2,1)} %bitcast.25, bf16[256,128]{1,0:T(8,128)(2,1)} %bitcast.26), kind=kLoop, calls=%fused_computation.1 | loop fusion | flops 589824 | bytes 393216 | tf_op jit(solution)/shard_map/concatenate | solution.py:309
  0.9 0.1 shard_map.100.pack.refs_4_
  1.0 4.8 %collective-permute-start = (bf16[640,128]{1,0:T(8,128)(2,1)S(1)}, bf16[640,128]{1,0:T(8,128)(2,1)S(1)}, u32[]{:S(2)}, u32[]{:S(2)}) collective-permute-start(bf16[640,128]{1,0:T(8,128)(2,1)S(1)} %shard_map.100.pack.refs_4_), channel_id=1, source_target_pairs={{0,16},{8,24},{16,32},{24,40},{32,48},{40,56},{48,64},{56,72},{64,... | collective-permute-start | bytes 491528 | tf_op jit(solution)/shard_map/ppermute | solution.py:312
  5.9 1.3 %pad_maximum_fusion.both.queries.refs_1_ = bf16[512,1024]{1,0:T(8,128)(2,1)S(1)} fusion(bf16[256,1024]{1,0:T(8,128)(2,1)} %bitcast.22, bf16[256,1024]{1,0:T(8,128)(2,1)} %bitcast.23), kind=kLoop, calls=%fused_computation | loop fusion | flops 2097152 | bytes 2097152 | tf_op jit(solution)/shard_map/concatenate | solution.py:316
  7.1 6.6 %collective-permute-start.2 = (bf16[640,128]{1,0:T(8,128)(2,1)S(1)}, bf16[640,128]{1,0:T(8,128)(2,1)S(1)}, u32[]{:S(2)}, u32[]{:S(2)}) collective-permute-start(bf16[640,128]{1,0:T(8,128)(2,1)S(1)} %shard_map.100.pack.refs_4_), channel_id=1, source_target_pairs={{0,8},{8,32},{16,24},{24,48},{32,40},{40,64},{48,56},{56,80},{64,7... | collective-permute-start | bytes 491528 | tf_op jit(solution)/shard_map/ppermute | solution.py:318
  13.8 0.0 copy-done.3
  13.8 0.0 copy-done.4
  13.8 0.1 add_bitcast_fusion.spot
  13.9 1.2 %shard_map.101 = (f32[8,256,256]{2,1,0:T(8,128)S(1)}, f32[8,256,256]{2,1,0:T(8,128)S(1)}, f32[8,8,256]{2,1,0:T(8,128)S(1)}, bf16[256,1024]{1,0:T(8,128)(2,1)S(1)}, s32[8,256]{1,0:T(8,128)S(1)}) custom-call(s32[1,6]{1,0:T(1,128)S(1)} %add_bitcast_fusion.spot, bf16[512,1024]{1,0:T(8,128)(2,1)S(1)} %pad_maximum_fusion.both.queries.refs_1_, ...), custom_call_target="tpu_custom_call" | custom-call | flops 268435456 | bytes 1048576 | tf_op jit(solution)/shard_map/pallas_call | solution.py:324
  15.1 0.0 collective-permute-done.pack.refs_5_
  15.1 1.9 %collective-permute-start.1 = (bf16[640,128]{1,0:T(8,128)(2,1)S(1)}, bf16[640,128]{1,0:T(8,128)(2,1)S(1)}, u32[]{:S(2)}, u32[]{:S(2)}) collective-permute-start(bf16[640,128]{1,0:T(8,128)(2,1)S(1)} %collective-permute-done.pack.refs_5_), channel_id=1, source_target_pairs={{0,8},{8,0},{1,9},{9,1},{2,10},{10,2},{3,11},{11,3},{4,12},{12,4},... | collective-permute-start | bytes 491528 | tf_op jit(solution)/shard_map/ppermute | solution.py:329
  17.0 1.0 %shard_map.102 = (f32[8,256,256]{2,1,0:T(8,128)S(1)}, f32[8,256,256]{2,1,0:T(8,128)S(1)}, f32[8,8,256]{2,1,0:T(8,128)S(1)}) custom-call(s32[8,256]{1,0:T(8,128)S(1)} %get-tuple-element.20.place.refs_0_, bf16[512,1024]{1,0:T(8,128)(2,1)S(1)} %pad_maximum_fusion.both.queries.refs_1_, bf16[256,1024]{1,0:T(8,128)(2,1)S(1)} %get-tuple-element.21.cotangent.refs_2_, ...), custom_call_target="tpu_custom_call" | custom-call | flops 268435456 | bytes 1048576 | tf_op jit(solution)/shard_map/pallas_call | solution.py:330
  18.0 0.0 collective-permute-done.2.refs_7_
  18.0 0.4 collective-permute-done.1.refs_6_
  18.4 0.0 copy-start
  18.4 0.0 copy-start.1
  18.4 5.7 %shard_map.103 = (f32[32,1152]{1,0:T(8,128)S(1)}, bf16[32,1152]{1,0:T(8,128)(2,1)S(1)}) custom-call(s32[8,256]{1,0:T(8,128)S(1)} %get-tuple-element.20.place.refs_0_, bf16[512,1024]{1,0:T(8,128)(2,1)S(1)} %pad_maximum_fusion.both.queries.refs_1_, bf16[256,1024]{1,0:T(8,128)(2,1)S(1)} %get-tuple-element.21.cotangent.refs_2_, ...), custom_call_target="tpu_custom_call" | custom-call | flops 2147483648 | bytes 1048576 | tf_op jit(solution)/shard_map/pallas_call | solution.py:336
  24.0 0.0 copy-start.2
  24.1 1.9 %all_gather.3.got_ref = bf16[64,1152]{1,0:T(8,128)(2,1)S(1)} all-gather(bf16[32,1152]{1,0:T(8,128)(2,1)S(1)} %get-tuple-element.32), channel_id=1, replica_groups=mesh['y'=4,'z'=8,'core'=2,'tp'=4,'seq'=2] {'core'}, dimensions={0}, use_global_device_ids=true | all-gather | bytes 221184 | tf_op jit(solution)/shard_map/all_gather | solution.py:353
  26.0 0.2 shard_map.104
  26.1 27.5 %all_to_all.15 = bf16[64,2,640]{2,1,0:T(2,128)(2,1)S(1)} all-to-all(bf16[64,2,640]{2,1,0:T(2,128)(2,1)S(1)} %bitcast.17), channel_id=1, replica_groups=mesh['y'=4,'z'=8,'core'=2,'tp'=4,'seq'=2] {'z','y','seq'}, dimensions={0} | all-to-all | bytes 327680 | tf_op jit(solution)/shard_map/all_to_all | solution.py:357
  53.7 0.0 copy-done
  53.7 0.0 copy-done.1
  53.7 0.5 shard_map.105
  54.2 12.1 %all_to_all.16.in_ref = f32[16,1,640]{2,1,0:T(1,128)S(1)} all-to-all(f32[16,1,640]{2,1,0:T(1,128)S(1)} %shard_map.105), channel_id=1, replica_groups=mesh['y'=4,'z'=8,'core'=2,'tp'=4,'seq'=2] {'z','core'}, dimensions={0} | all-to-all | bytes 81920 | tf_op jit(solution)/shard_map/all_to_all | solution.py:363
  66.3 13.5 %all_to_all.17 = f32[32,1,640]{2,1,0:T(1,128)S(1)} all-to-all(f32[32,1,640]{2,1,0:T(1,128)S(1)} %shard_map.106), channel_id=1, replica_groups=mesh['y'=4,'z'=8,'core'=2,'tp'=4,'seq'=2] {'tp','y','seq'}, dimensions={0} | all-to-all | bytes 163840 | tf_op jit(solution)/shard_map/all_to_all | solution.py:365
  79.8 0.0 copy-done.2
  79.8 0.9 %shard_map.107 = f32[2,512]{1,0:T(2,128)} custom-call(f32[16,2,1,640]{3,2,1,0:T(1,128)S(1)} %bitcast.19, s32[1,512]{1,0:T(1,128)S(1)} %bitcast.21), custom_call_target="tpu_custom_call" | custom-call | bytes 1048576 | tf_op jit(solution)/shard_map/pallas_call | solution.py:366
  (1 shorter events, 0.0 us)
Async XLA Ops:
  0.0 13.8 %copy-start.3 = (s32[2]{0:T(128)S(1)}, s32[2]{0:T(128)}, u32[]{:S(2)}) copy-start(s32[2]{0:T(128)} %param.16) | copy-start | bytes 28
  0.0 13.8 %copy-start.4 = (s32[2]{0:T(128)S(1)}, s32[2]{0:T(128)}, u32[]{:S(2)}) copy-start(s32[2]{0:T(128)} %param.15) | copy-start | bytes 28
  1.0 14.0 %collective-permute-start = (bf16[640,128]{1,0:T(8,128)(2,1)S(1)}, bf16[640,128]{1,0:T(8,128)(2,1)S(1)}, u32[]{:S(2)}, u32[]{:S(2)}) collective-permute-start(bf16[640,128]{1,0:T(8,128)(2,1)S(1)} %shard_map.100.pack.refs_4_), channel_id=1, source_target_pairs={{0,16},{8,24},{16,32},{24,40},{32,48},{40,56},{48,64},{56,72},{64,... | collective-permute-start | bytes 491528 | tf_op jit(solution)/shard_map/ppermute | solution.py:312
  7.1 10.8 %collective-permute-start.2 = (bf16[640,128]{1,0:T(8,128)(2,1)S(1)}, bf16[640,128]{1,0:T(8,128)(2,1)S(1)}, u32[]{:S(2)}, u32[]{:S(2)}) collective-permute-start(bf16[640,128]{1,0:T(8,128)(2,1)S(1)} %shard_map.100.pack.refs_4_), channel_id=1, source_target_pairs={{0,8},{8,32},{16,24},{24,48},{32,40},{40,64},{48,56},{56,80},{64,7... | collective-permute-start | bytes 491528 | tf_op jit(solution)/shard_map/ppermute | solution.py:318
  15.1 3.3 %collective-permute-start.1 = (bf16[640,128]{1,0:T(8,128)(2,1)S(1)}, bf16[640,128]{1,0:T(8,128)(2,1)S(1)}, u32[]{:S(2)}, u32[]{:S(2)}) collective-permute-start(bf16[640,128]{1,0:T(8,128)(2,1)S(1)} %collective-permute-done.pack.refs_5_), channel_id=1, source_target_pairs={{0,8},{8,0},{1,9},{9,1},{2,10},{10,2},{3,11},{11,3},{4,12},{12,4},... | collective-permute-start | bytes 491528 | tf_op jit(solution)/shard_map/ppermute | solution.py:329
  18.4 35.3 %copy-start = (f32[256,1,1024]{2,1,0:T(1,128)S(1)}, f32[256,1,1024]{2,1,0:T(1,128)}, u32[]{:S(2)}) copy-start(f32[256,1,1024]{2,1,0:T(1,128)} %param.18) | copy-start | bytes 3145732
  18.4 35.3 %copy-start.1 = (f32[256,1,128]{2,1,0:T(1,128)S(1)}, f32[256,1,128]{2,1,0:T(1,128)}, u32[]{:S(2)}) copy-start(f32[256,1,128]{2,1,0:T(1,128)} %param.19) | copy-start | bytes 393220
  24.0 55.8 %copy-start.2 = (s32[512]{0:T(512)S(1)}, s32[512]{0:T(512)}, u32[]{:S(2)}) copy-start(s32[512]{0:T(512)} %param.17) | copy-start | bytes 6148
